TPU v7x, 256 devices: a whole 4x4x8 slice. The times are simulated.
256 devices in a mesh: wide: 32 (over x, z), narrow: 8 (over y, core).
Axes of the slice: x: 4, y: 4, z: 8, core: 2. Of those that a mesh axis runs over, the one named last changes fastest.
Arguments:
- hidden: bfloat16 [8192, 5120], P('wide', 'narrow'), may hold values from -6 to 6
- resid: bfloat16 [8192, 5120], P('wide'), may hold values from -6 to 6
- w_out: bfloat16 [5120, 5120], P('narrow', 'wide'), may hold values from -0.078125 to 0.078125
- key_gain: bfloat16 [5120], P('narrow'), may hold values from 0.099609375 to 1.8984375
- cluster_ids: int32 [8192], P('wide'), may hold values from 0 to 32767, as said below
- centroids: bfloat16 [32768, 5120], P(('wide', 'narrow')), may hold values from -6 to 6
- rotation: bfloat16 [5120, 5120], P(None, 'narrow'), may hold values from -0.078125 to 0.078125
Outputs:
- rotated: bfloat16 [32768, 5120], P('wide', 'narrow')
Inputs may be any that keep to these rules, and one draw needn't show every extreme that they name: `cluster_ids`: in each block of 256 tokens at most 32 tokens have clusters of one owner (owner = id // 1024); one owner, the same for every block, gets exactly 32 tokens from every block; the other 224 tokens of a block are spread as evenly as possible over the other owners, so their counts differ by at most one.
All inputs are finite; a program needn't handle non-finite values.
Results may differ from a plain program's by a relative error of at most 0.0055.
Values may be sent and summed in bfloat16 or wider, within the bound.
No kernel may reach another device: no remote copies, remote signals or barrier semaphores. Data moves between devices by JAX's collectives and lax.ppermute only.
A program may use at most 64 MiB of HBM per device.

v0:
```python
import jax
import jax.numpy as jnp
from jax import lax
from jax.sharding import PartitionSpec as P

CL_DEV = 1024


EPS = 1e-05


def per_device(hidden, resid, w_out, key_gain, cluster_ids, centroids, rotation):
    wide_count = lax.axis_size("wide")
    width_local = hidden.shape[1]
    token_count = hidden.shape[0]
    partial_sum = jnp.dot(
        hidden,
        lax.all_gather(w_out, "wide", axis=1, tiled=True),
        preferred_element_type=jnp.float32,
    )
    col_start = lax.axis_index("narrow") * width_local
    summed = lax.psum(partial_sum, "narrow")
    stream = resid.astype(jnp.float32) + summed
    norm_scale = lax.rsqrt(jnp.mean(stream * stream, axis=1, keepdims=True) + EPS)
    stream_part = lax.dynamic_slice_in_dim(stream, col_start, width_local, 1)
    key_rows = (stream_part * norm_scale * key_gain.astype(jnp.float32)[None, :]).astype(
        jnp.bfloat16
    )
    capacity = 4 * token_count // wide_count
    owner_of = cluster_ids // CL_DEV
    owners = jnp.arange(wide_count, dtype=jnp.int32)
    onehot = (owner_of[:, None] == owners[None, :]).astype(jnp.int32)
    slot_rank = jnp.sum((jnp.cumsum(onehot, axis=0) - onehot) * onehot, axis=1)
    target = owner_of * capacity + slot_rank
    send_keys = (
        jnp.zeros((wide_count * capacity, width_local), jnp.bfloat16).at[target].set(key_rows)
    )
    send_ids = jnp.full((wide_count * capacity,), -1, jnp.int32).at[target].set(cluster_ids)
    got_keys, got_ids = (
        lax.all_to_all(send_keys, "wide", split_axis=0, concat_axis=0, tiled=True),
        lax.all_to_all(send_ids, "wide", split_axis=0, concat_axis=0, tiled=True),
    )
    centroid_tiles = lax.all_to_all(centroids, "narrow", split_axis=1, concat_axis=0, tiled=True)
    local_id = got_ids - lax.axis_index("wide") * CL_DEV
    filled = got_ids >= 0
    centre_rows = jnp.take(centroid_tiles, jnp.clip(local_id, 0, CL_DEV - 1), axis=0).astype(
        jnp.float32
    )
    residual = (got_keys.astype(jnp.float32) - jnp.where(filled[:, None], centre_rows, 0.0)).astype(
        jnp.bfloat16
    )
    rotated = jnp.dot(
        lax.all_gather(residual, "narrow", axis=1, tiled=True),
        rotation,
        preferred_element_type=jnp.float32,
    )
    return rotated.astype(jnp.bfloat16)


def solution(mesh):
    placed = (
        P("wide", "narrow"),
        P("wide", None),
        P("narrow", "wide"),
        P("narrow"),
        P("wide"),
        P(("wide", "narrow"), None),
        P(None, "narrow"),
    )
    return jax.shard_map(
        per_device, mesh=mesh, in_specs=placed, out_specs=P("wide", "narrow"), check_vma=False
    )
```

profile of v0, /device:TPU:8, one launch (start us, length us, event | category | flops | bytes accessed | tf_op | source)
XLA Modules:
  0.0 335.9 jit_solution(7304214924513392886)
XLA Ops:
  6.5 0.7 all-gather.3.cloned.1.call-update
  7.3 0.0 all-reduce.2.cloned.1.call-start
  7.3 95.2 %all-gather.3.cloned.1.call-done = bf16[640,5120]{0,1:T(8,128)(2,1)} async-done(((bf16[640,160]{0,1:T(8,128)(2,1)}), bf16[640,5120]{0,1:T(8,128)(2,1)}) %all-gather.3.cloned.1.call-update) | async-done | bytes 6553616 | tf_op jit(solution)/shard_map/all_gather | solution.py:18
  102.5 7.5 %fusion.12 = f32[256,5120]{1,0:T(8,128)} fusion(bf16[256,640]{1,0:T(8,128)(2,1)S(1)} %copy-done, bf16[640,5120]{0,1:T(8,128)(2,1)} %all-gather.3.cloned.1.call-done), kind=kOutput, calls=%fused_computation.38 | convolution fusion | flops 1677721600 | bytes 12124160 | tf_op jit(solution)/shard_map/dot_general | solution.py:16
  110.0 0.0 all-reduce.2.cloned.1.call-update
  110.0 0.7 copy-done.2
  110.7 0.6 reduce-window.6
  111.3 0.2 slice_reduce_fusion
  111.5 0.1 fusion.7
  111.6 1.4 scatter_custom_fusion.1
  113.1 0.7 all_to_all.28
  113.7 5.7 %all-to-all-start.1 = ((s32[32,32,1]{1,2,0:T(1,128)}), s32[32,32,1]{1,2,0:T(1,128)S(1)}, u32[]{:S(2)}, u32[]{:S(2)}) async-start(s32[32,32,1]{1,2,0:T(1,128)} %bitcast.4), calls=%async_computation.1 | async-start | bytes 32768 | tf_op jit(solution)/shard_map/all_to_all | solution.py:41
  119.5 1.2 copy.18
  120.7 8.5 %all-to-all-done.1 = s32[32,32,1]{1,2,0:T(1,128)S(1)} async-done(((s32[32,32,1]{1,2,0:T(1,128)}), s32[32,32,1]{1,2,0:T(1,128)S(1)}, u32[]{:S(2)}, u32[]{:S(2)}) %all-to-all-start.1) | async-done | bytes 4128 | tf_op jit(solution)/shard_map/all_to_all | solution.py:41
  129.2 4.8 %all-to-all-start.2 = ((bf16[128,8,640]{2,0,1:T(8,128)(2,1)}), bf16[128,8,640]{2,0,1:T(8,128)(2,1)S(1)}, u32[]{:S(2)}, u32[]{:S(2)}) async-start(bf16[128,8,640]{2,0,1:T(8,128)(2,1)} %bitcast.39), calls=%async_computation.2 | async-start | bytes 2621440 | tf_op jit(solution)/shard_map/all_to_all | solution.py:43
  134.0 65.9 %all-reduce.2.cloned.1.call-done = f32[256,5120]{1,0:T(8,128)} async-done(((f32[256,5120]{1,0:T(8,128)}), f32[256,5120]{1,0:T(8,128)}) %all-reduce.2.cloned.1.call-update) | async-done | bytes 5242896 | tf_op jit(solution)/shard_map/psum | solution.py:22
  199.9 6.4 %multiply_reduce_fusion = (f32[256]{0:T(256)S(1)}, f32[256,5120]{1,0:T(8,128)}) fusion(f32[256,5120]{1,0:T(8,128)} %all-reduce.2.cloned.1.call-done, bf16[256,5120]{1,0:T(8,128)(2,1)} %param.8), kind=kLoop, calls=%fused_computation.3 | loop fusion | flops 5242624 | bytes 13108224 | tf_op jit(solution)/shard_map/reduce_sum | solution.py:24
  206.3 3.4 %scatter_custom_fusion = bf16[1024,640]{1,0:T(8,128)(2,1)} fusion(s32[256]{0:T(256)S(1)} %compare_select_fusion.2, bf16[]{:T(256)} %constant.24.clone.1, f32[256,5120]{1,0:T(8,128)} %get-tuple-element.8, s32[]{:T(128)} %constant.26.clone.1, s32[]{:T(128)S(6)} %select_n.38, f32[640]{0:T(1024)S(1)} %convert_element_type.34, f32[256]{0:T(256)S(1)} %add_rsqrt_fusion), kind=kCustom, calls=%fused_computation.10 | custom fusion | flops 491520 | bytes 1972228 | tf_op jit(solution)/shard_map/scatter | solution.py:36
  209.7 10.0 %all-to-all-start = ((bf16[32,32,640]{2,1,0:T(8,128)(2,1)}), bf16[32,32,640]{2,1,0:T(8,128)(2,1)S(1)}, u32[]{:S(2)}, u32[]{:S(2)}) async-start(bf16[32,32,640]{2,1,0:T(8,128)(2,1)} %bitcast.41), calls=%async_computation | async-start | bytes 2621440 | tf_op jit(solution)/shard_map/all_to_all | solution.py:40
  219.6 0.0 all-gather.5.cloned.1.call-start
  219.7 0.6 broadcast.123
  220.3 0.8 fusion.11
  221.0 0.1 min.18
  221.1 0.1 min.16
  221.2 0.1 compare_reduce_fusion
  221.3 0.1 ge.28
  221.4 5.1 %gather_fusion = bf16[1024,640]{1,0:T(8,128)(2,1)} fusion(bf16[1024,640]{1,0:T(8,128)(2,1)S(1)} %bitcast.40, s32[1024]{0:T(1024)S(1)} %broadcast_clamp_fusion), kind=kCustom, calls=%fused_computation | custom fusion | bytes 2625536 | tf_op jit(solution)/shard_map/jit(_take)/gather | solution.py:46
  226.5 27.8 %all-to-all-done = bf16[32,32,640]{2,1,0:T(8,128)(2,1)S(1)} async-done(((bf16[32,32,640]{2,1,0:T(8,128)(2,1)}), bf16[32,32,640]{2,1,0:T(8,128)(2,1)S(1)}, u32[]{:S(2)}, u32[]{:S(2)}) %all-to-all-start) | async-done | bytes 1310752 | tf_op jit(solution)/shard_map/all_to_all | solution.py:40
  254.3 2.9 fusion
  257.1 0.0 all-gather.5.cloned.1.call-update
  257.2 58.5 %all-gather.5.cloned.1.call-done = bf16[1024,5120]{1,0:T(8,128)(2,1)} async-done(((bf16[1024,640]{1,0:T(8,128)(2,1)}), bf16[1024,5120]{1,0:T(8,128)(2,1)}) %all-gather.5.cloned.1.call-update) | async-done | bytes 10485776 | tf_op jit(solution)/shard_map/all_gather | solution.py:53
  315.6 13.7 %convolution_convert_fusion = bf16[1024,640]{1,0:T(8,128)(2,1)} fusion(bf16[1024,5120]{1,0:T(8,128)(2,1)} %all-gather.5.cloned.1.call-done, bf16[5120,640]{1,0:T(8,128)(2,1)} %param.13), kind=kOutput, calls=%fused_computation.7 | convolution fusion | flops 6711541760 | bytes 18350080 | tf_op jit(solution)/shard_map/dot_general | solution.py:52
  (20 shorter events, 0.1 us)
Async XLA Ops:
  6.5 96.0 %copy-start = (bf16[256,640]{1,0:T(8,128)(2,1)S(1)}, bf16[256,640]{1,0:T(8,128)(2,1)}, u32[]{:S(2)}) copy-start(bf16[256,640]{1,0:T(8,128)(2,1)} %param.7) | copy-start | bytes 983044
  6.5 96.0 %all-gather.3.cloned.1.call-start = ((), (), s32[]{:S(2)}) async-start(), calls=%async_computation.3 | async-start | bytes 6758400 | tf_op jit(solution)/shard_map/all_gather | solution.py:18
  7.3 192.6 %all-reduce.2.cloned.1.call-start = ((), (), s32[]{:S(2)}) async-start(), calls=%async_computation.4 | async-start | bytes 10485760 | tf_op jit(solution)/shard_map/psum | solution.py:22
  110.0 0.7 copy-start.2
  110.0 9.5 %copy-start.1 = (bf16[128,5120]{1,0:T(8,128)(2,1)S(1)}, bf16[128,5120]{1,0:T(8,128)(2,1)}, u32[]{:S(2)}) copy-start(bf16[128,5120]{1,0:T(8,128)(2,1)} %param.12) | copy-start | bytes 3932164
  113.7 15.4 %all-to-all-start.1 = ((s32[32,32,1]{1,2,0:T(1,128)}), s32[32,32,1]{1,2,0:T(1,128)S(1)}, u32[]{:S(2)}, u32[]{:S(2)}) async-start(s32[32,32,1]{1,2,0:T(1,128)} %bitcast.4), calls=%async_computation.1 | async-start | bytes 32768 | tf_op jit(solution)/shard_map/all_to_all | solution.py:41
  119.5 14.5 %copy-start.3 = (bf16[640]{0:T(1024)(128)(2,1)S(1)}, bf16[640]{0:T(1024)(128)(2,1)}, u32[]{:S(2)}) copy-start(bf16[640]{0:T(1024)(128)(2,1)} %param.10) | copy-start | bytes 3844
  129.2 80.5 %all-to-all-start.2 = ((bf16[128,8,640]{2,0,1:T(8,128)(2,1)}), bf16[128,8,640]{2,0,1:T(8,128)(2,1)S(1)}, u32[]{:S(2)}, u32[]{:S(2)}) async-start(bf16[128,8,640]{2,0,1:T(8,128)(2,1)} %bitcast.39), calls=%async_computation.2 | async-start | bytes 2621440 | tf_op jit(solution)/shard_map/all_to_all | solution.py:43
  209.7 44.6 %all-to-all-start = ((bf16[32,32,640]{2,1,0:T(8,128)(2,1)}), bf16[32,32,640]{2,1,0:T(8,128)(2,1)S(1)}, u32[]{:S(2)}, u32[]{:S(2)}) async-start(bf16[32,32,640]{2,1,0:T(8,128)(2,1)} %bitcast.41), calls=%async_computation | async-start | bytes 2621440 | tf_op jit(solution)/shard_map/all_to_all | solution.py:40
  219.6 96.0 %all-gather.5.cloned.1.call-start = ((), (), s32[]{:S(2)}) async-start(), calls=%async_computation.5 | async-start | bytes 11796480 | tf_op jit(solution)/shard_map/all_gather | solution.py:53
Sparse Core Ops, SparseCore 0:
  9.9 92.5 all-gather.2
  110.1 89.7 all-reduce.1
  257.3 58.2 all-gather.4
where the time goes:
time: 338 us; the launch traced here: 336 us
  waiting for transfers between devices  257 us (76%)
  matrix products  21.2 us (6%)
  starting transfers between devices  20.6 us (6%)
  other arithmetic  14.2 us (4%)
  between operations  13.2 us (4%)
  local copies, waits for them, and re-layouts  10.1 us (3%)
    all_gather x1, waiting for transfers between devices, per_device(): lax.all_gather(w_out, 'wide', axis=1, tiled=True)  95.2 us
    psum x1, waiting for transfers between devices, per_device(): summed = lax.psum(partial_sum, 'narrow')  65.9 us
    all_gather x1, waiting for transfers between devices, per_device(): lax.all_gather(residual, 'narrow', axis=1, tiled=True)  58.5 us
    all_to_all x1, waiting for transfers between devices, per_device(): lax.all_to_all(send_keys, 'wide', split_axis=0, concat_axis=0, tiled=True)  27.8 us
    dot_general x1, matrix products, per_device(): jnp.dot(lax.all_gather(residual, 'narrow', axis=1, tiled=True), rotation,...  13.7 us
    all_to_all x1, starting transfers between devices, per_device(): lax.all_to_all(send_keys, 'wide', split_axis=0, concat_axis=0, tiled=True)  9.97 us
    all_to_all x1, waiting for transfers between devices, per_device(): lax.all_to_all(send_ids, 'wide', split_axis=0, concat_axis=0, tiled=True)  8.5 us
    dot_general x1, matrix products, per_device(): jnp.dot(hidden, lax.all_gather(w_out, 'wide', axis=1, tiled=True), prefer...  7.47 us
  transfers between devices with their start and end apart: 6, of which 5 were waited for; matrix products, arithmetic and copies ran while one was open for 6% of the time, Pallas kernels for 0%

commit v1 on v0

v1 whole, which is shorter than its diff:
```python
import jax
import jax.numpy as jnp
from jax import lax
from jax.sharding import Mesh, PartitionSpec as P

CL_DEV = 1024
EPS = 1e-05
NX, NZ, NY, NC = 4, 8, 4, 2
WIDE = ("x", "z")
NARROW = ("y", "c")
BF = jnp.bfloat16
F32 = jnp.float32


def shifted(a, axis, n, h):
    return lax.ppermute(a, axis, [(i, (i + h) % n) for i in range(n)])


def pick(a, i, axis=0):
    return lax.dynamic_index_in_dim(a, i, axis, keepdims=False)


def per_device(hidden, resid, w_out, key_gain, cluster_ids, centroids, rotation):
    xi, zi, yi, ci = (lax.axis_index(a) for a in ("x", "z", "y", "c"))
    ni = yi * NC + ci
    wi = xi * NZ + zi
    tokens, width = hidden.shape
    n_wide, n_narrow = NX * NZ, NY * NC
    d = width * n_narrow
    cap = 4 * tokens // n_wide
    slots = n_wide * cap
    rows = tokens // n_narrow
    cols = w_out.shape[1]

    owner_of = cluster_ids // CL_DEV
    onehot = (owner_of[:, None] == jnp.arange(n_wide, dtype=jnp.int32)[None, :]).astype(jnp.int32)
    rank = jnp.sum((jnp.cumsum(onehot, axis=0) - onehot) * onehot, axis=1)
    target = owner_of * cap + rank
    slot_of = target[:, None] == jnp.arange(slots, dtype=jnp.int32)[None, :]
    send_ids = jnp.sum(jnp.where(slot_of, cluster_ids[:, None] + 1, 0), axis=0) - 1
    got_ids = lax.all_to_all(send_ids, WIDE, 0, 0, tiled=True)

    w_t = w_out.T
    w_parts = [w_t] + [shifted(w_t, "z", NZ, -h) for h in (1, 2, 3, 4, 5, 6, 7)]
    h_parts = [hidden] + [shifted(hidden, "x", NX, h) for h in (1, 2, 3)]
    w_all = jnp.zeros((NZ * cols, width), BF)
    for h, part in enumerate(w_parts):
        w_all = lax.dynamic_update_slice(w_all, part, (((zi + h) % NZ) * cols, 0))
    wide_cols = NZ * cols

    cent_tile = lax.all_to_all(centroids, NARROW, split_axis=1, concat_axis=0, tiled=True)
    local_id = jnp.where(got_ids >= 0, got_ids - wi * CL_DEV, -1)
    choose = (local_id[:, None] == jnp.arange(CL_DEV, dtype=jnp.int32)[None, :]).astype(BF)
    cent_send = jnp.dot(choose, cent_tile, preferred_element_type=F32).astype(BF)
    cent_slots = lax.all_to_all(cent_send, WIDE, 0, 0, tiled=True)
    cent_tok = jnp.dot(slot_of.astype(BF), cent_slots, preferred_element_type=F32).astype(BF)
    cent_rows = lax.all_to_all(cent_tok.reshape(n_narrow, rows, width), NARROW, 0, 0, tiled=True)
    cent_rows = cent_rows.transpose(1, 0, 2).reshape(rows, d)

    partial = jnp.stack(
        [
            lax.dot_general(p, w_all, (((1,), (1,)), ((), ())), preferred_element_type=F32)
            for p in h_parts
        ]
    ).astype(BF)
    partial = partial.reshape(NX, NY, NC, rows, wide_cols)
    other = shifted(pick(partial, 1 - ci, 2), "c", NC, 1)
    pair = (pick(partial, ci, 2).astype(F32) + other.astype(F32)).astype(BF)
    total = pick(pair, yi, 1).astype(F32)
    for h in (1, 2, 3):
        total = total + shifted(pick(pair, (yi + h) % NY, 1), "y", NY, h).astype(F32)
    total = total.astype(BF)
    back = jnp.stack([total[0]] + [shifted(total[h], "x", NX, -h) for h in (1, 2, 3)])
    projected = jnp.concatenate([pick(back, (j - xi) % NX) for j in range(NX)], axis=1)

    stream = (
        lax.dynamic_slice_in_dim(resid, ni * rows, rows, 0).astype(F32) + projected.astype(F32)
    )
    norm_scale = lax.rsqrt(jnp.mean(stream * stream, axis=1, keepdims=True) + EPS)
    gain = lax.all_gather(key_gain, NARROW, axis=0, tiled=True)
    key_rows = (stream * norm_scale * gain.astype(F32)[None, :]).astype(BF)
    residual = (key_rows.astype(F32) - cent_rows.astype(F32)).astype(BF)

    same = jnp.stack([residual] + [shifted(residual, "y", NY, h) for h in (1, 2, 3)])
    both = [same, shifted(same, "c", NC, 1)]
    k_of = jnp.arange(NC)[:, None, None]
    h_of = jnp.arange(NY)[None, :, None]
    r_of = jnp.arange(rows)[None, None, :]
    token_of = (((yi - h_of) % NY) * NC + (ci + k_of) % NC) * rows + r_of
    rotated = jnp.concatenate(
        [
            jnp.dot(b.reshape(NY * rows, d), rotation, preferred_element_type=F32).astype(BF)
            for b in both
        ]
    )
    place = jnp.take(target, token_of.reshape(-1))
    pack = (jnp.arange(slots, dtype=jnp.int32)[:, None] == place[None, :]).astype(BF)
    packed = jnp.dot(pack, rotated, preferred_element_type=F32).astype(BF)
    return lax.all_to_all(packed, WIDE, 0, 0, tiled=True)


def solution(mesh):
    grid = Mesh(mesh.devices.reshape(NX, NZ, NY, NC), ("x", "z", "y", "c"))
    placed = (
        P(WIDE, NARROW),
        P(WIDE, None),
        P(NARROW, WIDE),
        P(NARROW),
        P(WIDE),
        P(WIDE + NARROW, None),
        P(None, NARROW),
    )
    return jax.shard_map(
        per_device, mesh=grid, in_specs=placed, out_specs=P(WIDE, NARROW), check_vma=False
    )
```

time: 338 us -> 233 us (0.69)
  waiting for transfers between devices: 257 us -> 66 us
  blocking collectives: 0 us -> 56.8 us
  starting transfers between devices: 20.6 us -> 61.2 us
  between operations: 13.2 us -> 0.59 us
  local copies, waits for them, and re-layouts: 10.1 us -> 14.5 us
  other arithmetic: 14.2 us -> 10.2 us
    all_gather x2 -> x0, waiting for transfers between devices: 154 us -> none  [the longest x1 95.2 us: per_device(): lax.all_gather(w_out, 'wide', axis=1, tiled=True)]
    psum x1 -> x0, waiting for transfers between devices: 65.9 us -> none  [per_device(): summed = lax.psum(partial_sum, 'narrow')]
    ppermute x0 -> x21, waiting for transfers between devices: none -> 46.3 us  [shifted(): return lax.ppermute(a, axis, [(i, (i + h) % n) for i in range(n)])]
    all_to_all x0 -> x1, blocking collectives: none -> 43.2 us  [per_device(): return lax.all_to_all(packed, WIDE, 0, 0, tiled=True)]
    ppermute x0 -> x21, starting transfers between devices: none -> 35.2 us  [shifted(): return lax.ppermute(a, axis, [(i, (i + h) % n) for i in range(n)])]
    all_to_all x3 -> x4, waiting for transfers between devices: 36.3 us -> 19.7 us  [the longest x1 14.2 us: per_device(): lax.all_to_all(centroids, NARROW, split_axis=1, concat_axis=0, tiled=True)]
    all_gather x0 -> x1, blocking collectives: none -> 13.6 us  [per_device(): gain = lax.all_gather(key_gain, NARROW, axis=0, tiled=True)]
    all_to_all x3 -> x4, starting transfers between devices: 20.5 us -> 26 us  [the longest x1 9.16 us: per_device(): got_ids = lax.all_to_all(send_ids, WIDE, 0, 0, tiled=True)]
  transfers between devices with their start and end apart: 6 -> 25, of which waited for: 5 -> 12; matrix products, arithmetic and copies ran while one was open for 6% -> 15% of each run, Pallas kernels for 0% -> 0%
where the time goes in v1:
time: 233 us; the launch traced here: 230 us
  waiting for transfers between devices  66 us (28%)
  starting transfers between devices  61.2 us (26%)
  blocking collectives  56.8 us (24%)
  matrix products  21 us (9%)
  local copies, waits for them, and re-layouts  14.5 us (6%)
  other arithmetic  10.2 us (4%)
    ppermute x21, waiting for transfers between devices, shifted(): return lax.ppermute(a, axis, [(i, (i + h) % n) for i in range(n)])  46.3 us
    all_to_all x1, blocking collectives, per_device(): return lax.all_to_all(packed, WIDE, 0, 0, tiled=True)  43.2 us
    ppermute x21, starting transfers between devices, shifted(): return lax.ppermute(a, axis, [(i, (i + h) % n) for i in range(n)])  35.2 us
    all_to_all x1, waiting for transfers between devices, per_device(): lax.all_to_all(centroids, NARROW, split_axis=1, concat_axis=0, tiled=True)  14.2 us
    all_gather x1, blocking collectives, per_device(): gain = lax.all_gather(key_gain, NARROW, axis=0, tiled=True)  13.6 us
    all_to_all x1, starting transfers between devices, per_device(): got_ids = lax.all_to_all(send_ids, WIDE, 0, 0, tiled=True)  9.16 us
    all_to_all x1, starting transfers between devices, per_device(): cent_slots = lax.all_to_all(cent_send, WIDE, 0, 0, tiled=True)  7.49 us
    dot_general x2, matrix products, per_device(): jnp.dot(b.reshape(NY * rows, d), rotation, preferred_element_type=F32)  7.2 us
  transfers between devices with their start and end apart: 25, of which 12 were waited for; matrix products, arithmetic and copies ran while one was open for 15% of the time, Pallas kernels for 0%

profile of v1, /device:TPU:8, one launch (start us, length us, event | category | flops | bytes accessed | tf_op | source)
XLA Modules:
  0.0 230.3 jit_solution(13403728598315405400)
XLA Ops:
  0.0 5.9 %collective-permute-start = (bf16[160,640]{1,0:T(8,128)(2,1)}, bf16[160,640]{1,0:T(8,128)(2,1)}, u32[]{:S(2)}, u32[]{:S(2)}) collective-permute-start(bf16[160,640]{1,0:T(8,128)(2,1)} %bitcast.115), channel_id=1, source_target_pairs={{0,56},{8,0},{16,8},{24,16},{32,24},{40,32},{48,40},{56,48},{1,57}... | collective-permute-start | bytes 614408 | tf_op jit(solution)/shard_map/ppermute | solution.py:16
  7.8 5.0 %collective-permute-start.3 = (bf16[160,640]{1,0:T(8,128)(2,1)}, bf16[160,640]{1,0:T(8,128)(2,1)}, u32[]{:S(2)}, u32[]{:S(2)}) collective-permute-start(bf16[160,640]{1,0:T(8,128)(2,1)} %bitcast.118), channel_id=1, source_target_pairs={{0,32},{8,40},{16,48},{24,56},{32,0},{40,8},{48,16},{56,24},{1,33}... | collective-permute-start | bytes 614408 | tf_op jit(solution)/shard_map/ppermute | solution.py:16
  15.3 9.2 %all-to-all-start = ((s32[32,32,1]{1,2,0:T(1,128)}), s32[32,32,1]{1,2,0:T(1,128)S(1)}, u32[]{:S(2)}, u32[]{:S(2)}) async-start(s32[32,32,1]{1,2,0:T(1,128)} %bitcast.29), calls=%async_computation | async-start | bytes 32768 | tf_op jit(solution)/shard_map/all_to_all | solution.py:41
  26.2 2.7 %collective-permute-start.5 = (bf16[160,640]{1,0:T(8,128)(2,1)S(1)}, bf16[160,640]{1,0:T(8,128)(2,1)S(1)}, u32[]{:S(2)}, u32[]{:S(2)}) collective-permute-start(bf16[160,640]{1,0:T(8,128)(2,1)S(1)} %bitcast.120), channel_id=1, source_target_pairs={{0,16},{8,24},{16,32},{24,40},{32,48},{40,56},{48,0},{56,8},{1,17}... | collective-permute-start | bytes 614408 | tf_op jit(solution)/shard_map/ppermute | solution.py:16
  32.4 9.1 %collective-permute-done.2 = bf16[160,640]{1,0:T(8,128)(2,1)} collective-permute-done((bf16[160,640]{1,0:T(8,128)(2,1)}, bf16[160,640]{1,0:T(8,128)(2,1)}, u32[]{:S(2)}, u32[]{:S(2)}) %collective-permute-start.2) | collective-permute-done | bytes 204832 | tf_op jit(solution)/shard_map/ppermute | solution.py:16
  41.5 2.8 %collective-permute-start.9 = (bf16[256,640]{1,0:T(8,128)(2,1)}, bf16[256,640]{1,0:T(8,128)(2,1)S(1)}, u32[]{:S(2)}, u32[]{:S(2)}) collective-permute-start(bf16[256,640]{1,0:T(8,128)(2,1)} %param.7), channel_id=1, source_target_pairs={{0,192},{64,0},{128,64},{192,128},{1,193},{65,1},{129,65},{193,129... | collective-permute-start | bytes 983048 | tf_op jit(solution)/shard_map/ppermute | solution.py:16
  46.3 2.4 %collective-permute-start.8 = (bf16[256,640]{1,0:T(8,128)(2,1)S(1)}, bf16[256,640]{1,0:T(8,128)(2,1)S(1)}, u32[]{:S(2)}, u32[]{:S(2)}) collective-permute-start(bf16[256,640]{1,0:T(8,128)(2,1)S(1)} %copy-done.5), channel_id=1, source_target_pairs={{0,128},{64,192},{128,0},{192,64},{1,129},{65,193},{129,1},{193,65... | collective-permute-start | bytes 983048 | tf_op jit(solution)/shard_map/ppermute | solution.py:16
  50.7 7.0 %collective-permute-done.9 = bf16[256,640]{1,0:T(8,128)(2,1)S(1)} collective-permute-done((bf16[256,640]{1,0:T(8,128)(2,1)}, bf16[256,640]{1,0:T(8,128)(2,1)S(1)}, u32[]{:S(2)}, u32[]{:S(2)}) %collective-permute-start.9) | collective-permute-done | bytes 327712 | tf_op jit(solution)/shard_map/ppermute | solution.py:16
  59.2 2.8 %collective-permute-done.7 = bf16[256,640]{1,0:T(8,128)(2,1)S(1)} collective-permute-done((bf16[256,640]{1,0:T(8,128)(2,1)}, bf16[256,640]{1,0:T(8,128)(2,1)S(1)}, u32[]{:S(2)}, u32[]{:S(2)}) %collective-permute-start.7) | collective-permute-done | bytes 327712 | tf_op jit(solution)/shard_map/ppermute | solution.py:16
  65.1 5.0 %all-to-all-start.1 = ((bf16[128,8,640]{0,2,1:T(8,128)(2,1)}), bf16[128,8,640]{0,2,1:T(8,128)(2,1)}, u32[]{:S(2)}, u32[]{:S(2)}) async-start(bf16[128,8,640]{0,2,1:T(8,128)(2,1)} %bitcast.30), calls=%async_computation.1 | async-start | bytes 2621440 | tf_op jit(solution)/shard_map/all_to_all | solution.py:51
  70.2 1.8 pad_maximum_fusion
  73.4 14.2 %all-to-all-done.1 = bf16[128,8,640]{0,2,1:T(8,128)(2,1)} async-done(((bf16[128,8,640]{0,2,1:T(8,128)(2,1)}), bf16[128,8,640]{0,2,1:T(8,128)(2,1)}, u32[]{:S(2)}, u32[]{:S(2)}) %all-to-all-start.1) | async-done | bytes 1310752 | tf_op jit(solution)/shard_map/all_to_all | solution.py:51
  87.6 2.4 %copy.23 = bf16[8,128,640]{2,1,0:T(8,128)(2,1)} copy(bf16[8,128,640]{1,2,0:T(8,128)(2,1)} %bitcast.31) | data formatting | bytes 2621440 | tf_op jit(solution)/shard_map/all_to_all | solution.py:51
  90.0 4.4 %fusion.3 = bf16[1024,640]{1,0:T(8,128)(2,1)} fusion(bf16[1024,640]{1,0:T(8,128)(2,1)} %bitcast.106, s32[1024]{0:T(1024)S(1)} %select_n.234), kind=kOutput, calls=%fused_computation.11 | convolution fusion | flops 1343881216 | bytes 2625536 | tf_op jit(solution)/shard_map/dot_general | solution.py:54
  94.4 7.5 %all-to-all-start.2 = ((bf16[32,32,640]{2,1,0:T(8,128)(2,1)}), bf16[32,32,640]{2,1,0:T(8,128)(2,1)}, u32[]{:S(2)}, u32[]{:S(2)}) async-start(bf16[32,32,640]{2,1,0:T(8,128)(2,1)} %bitcast.104), calls=%async_computation.2 | async-start | bytes 2621440 | tf_op jit(solution)/shard_map/all_to_all | solution.py:55
  101.9 1.7 fusion.1
  104.8 3.5 %collective-permute-start.12 = (bf16[4,32,1280]{2,1,0:T(8,128)(2,1)S(1)}, bf16[4,32,1280]{2,1,0:T(8,128)(2,1)S(1)}, u32[]{:S(2)}, u32[]{:S(2)}) collective-permute-start(bf16[4,32,1280]{2,1,0:T(8,128)(2,1)S(1)} %get-tuple-element.7), channel_id=1, source_target_pairs={{0,4},{2,6},{4,0},{6,2},{1,5},{3,7},{5,1},{7,3},{8,12},{10,14},{12... | collective-permute-start | bytes 983048 | tf_op jit(solution)/shard_map/ppermute | solution.py:16
  108.9 6.6 %collective-permute-done.11 = bf16[4,32,1280]{2,1,0:T(8,128)(2,1)S(1)} collective-permute-done((bf16[4,32,1280]{2,1,0:T(8,128)(2,1)S(1)}, bf16[4,32,1280]{2,1,0:T(8,128)(2,1)S(1)}, u32[]{:S(2)}, u32[]{:S(2)}) %collective-permute-start.11) | collective-permute-done | bytes 327712 | tf_op jit(solution)/shard_map/ppermute | solution.py:16
  115.5 1.6 collective-permute-done.12
  117.1 5.3 %collective-permute-done.13 = bf16[4,32,1280]{2,1,0:T(8,128)(2,1)S(1)} collective-permute-done((bf16[4,32,1280]{2,1,0:T(8,128)(2,1)S(1)}, bf16[4,32,1280]{2,1,0:T(8,128)(2,1)S(1)}, u32[]{:S(2)}, u32[]{:S(2)}) %collective-permute-start.13) | collective-permute-done | bytes 327712 | tf_op jit(solution)/shard_map/ppermute | solution.py:16
  123.6 2.8 %collective-permute-start.14 = (bf16[32,1280]{1,0:T(8,128)(2,1)S(1)}, bf16[32,1280]{1,0:T(8,128)(2,1)S(1)}, u32[]{:S(2)}, u32[]{:S(2)}) collective-permute-start(bf16[32,1280]{1,0:T(8,128)(2,1)S(1)} %get-tuple-element.15), channel_id=1, source_target_pairs={{0,192},{64,0},{128,64},{192,128},{1,193},{65,1},{129,65},{193,129... | collective-permute-start | bytes 245768 | tf_op jit(solution)/shard_map/ppermute | solution.py:16
  128.1 13.6 %all-gather = bf16[8,1,640]{2,1,0:T(2,128)(2,1)S(1)} all-gather(bf16[1,1,640]{2,1,0:T(2,128)(2,1)S(1)} %reshape.246), channel_id=1, replica_groups=mesh['x'=4,'z'=8,'y'=4,'c'=2] {'y','c'}, dimensions={0}, use_global_device_ids=true | all-gather | bytes 11520 | tf_op jit(solution)/shard_map/all_gather | solution.py:80
  141.8 2.7 %convolution_convert_fusion.5 = bf16[256,640]{1,0:T(8,128)(2,1)} fusion(bf16[1024,640]{1,0:T(8,128)(2,1)} %bitcast.34, s32[256]{0:T(256)S(1)} %multiply_add_fusion), kind=kOutput, calls=%fused_computation.15 | convolution fusion | flops 335970304 | bytes 1639424 | tf_op jit(solution)/shard_map/dot_general | solution.py:56
  144.5 4.3 %all-to-all-start.3 = ((bf16[8,32,640]{2,1,0:T(8,128)(2,1)}), bf16[8,32,640]{2,1,0:T(8,128)(2,1)S(1)}, u32[]{:S(2)}, u32[]{:S(2)}) async-start(bf16[8,32,640]{2,1,0:T(8,128)(2,1)} %bitcast.35), calls=%async_computation.3 | async-start | bytes 655360 | tf_op jit(solution)/shard_map/all_to_all | solution.py:57
  150.0 5.5 %all-to-all-done.3 = bf16[8,32,640]{2,1,0:T(8,128)(2,1)S(1)} async-done(((bf16[8,32,640]{2,1,0:T(8,128)(2,1)}), bf16[8,32,640]{2,1,0:T(8,128)(2,1)S(1)}, u32[]{:S(2)}, u32[]{:S(2)}) %all-to-all-start.3) | async-done | bytes 327712 | tf_op jit(solution)/shard_map/all_to_all | solution.py:57
  156.9 3.5 %collective-permute-start.18 = (bf16[32,5120]{1,0:T(8,128)(2,1)S(1)}, bf16[32,5120]{1,0:T(8,128)(2,1)S(1)}, u32[]{:S(2)}, u32[]{:S(2)}) collective-permute-start(bf16[32,5120]{1,0:T(8,128)(2,1)S(1)} %subtract_convert_fusion), channel_id=1, source_target_pairs={{0,4},{2,6},{4,0},{6,2},{1,5},{3,7},{5,1},{7,3},{8,12},{10,14},{12... | collective-permute-start | bytes 983048 | tf_op jit(solution)/shard_map/ppermute | solution.py:16
  161.1 6.5 %collective-permute-done.17 = bf16[32,5120]{1,0:T(8,128)(2,1)S(1)} collective-permute-done((bf16[32,5120]{1,0:T(8,128)(2,1)S(1)}, bf16[32,5120]{1,0:T(8,128)(2,1)S(1)}, u32[]{:S(2)}, u32[]{:S(2)}) %collective-permute-start.17) | collective-permute-done | bytes 327712 | tf_op jit(solution)/shard_map/ppermute | solution.py:16
  169.2 5.3 %collective-permute-done.19 = bf16[32,5120]{1,0:T(8,128)(2,1)S(1)} collective-permute-done((bf16[32,5120]{1,0:T(8,128)(2,1)S(1)}, bf16[32,5120]{1,0:T(8,128)(2,1)S(1)}, u32[]{:S(2)}, u32[]{:S(2)}) %collective-permute-start.19) | collective-permute-done | bytes 327712 | tf_op jit(solution)/shard_map/ppermute | solution.py:16
  176.1 1.9 gather_fusion
  178.1 4.6 %convolution_convert_fusion.7 = bf16[128,640]{1,0:T(8,128)(2,1)S(1)} fusion(bf16[128,5120]{1,0:T(8,128)(2,1)} %bitcast.41, bf16[5120,640]{1,0:T(8,128)(2,1)} %param.13), kind=kOutput, calls=%fused_computation.17 | convolution fusion | flops 838942720 | bytes 8028160 | tf_op jit(solution)/shard_map/dot_general | solution.py:92
  182.8 2.6 %convolution_convert_fusion.6 = bf16[128,640]{1,0:T(8,128)(2,1)S(1)} fusion(bf16[128,5120]{1,0:T(8,128)(2,1)} %bitcast.42, bf16[5120,640]{1,0:T(8,128)(2,1)S(1)} %bitcast.101), kind=kOutput, calls=%fused_computation.16 | convolution fusion | flops 838942720 | bytes 8028160 | tf_op jit(solution)/shard_map/dot_general | solution.py:92
  186.0 43.2 %all_to_all.54 = bf16[32,32,640]{2,1,0:T(8,128)(2,1)S(1)} all-to-all(bf16[32,32,640]{2,1,0:T(8,128)(2,1)S(1)} %bitcast.105), channel_id=1, replica_groups=mesh['x'=4,'z'=8,'y'=4,'c'=2] {'x','z'}, dimensions={0} | all-to-all | bytes 2621440 | tf_op jit(solution)/shard_map/all_to_all | solution.py:99
  (97 shorter events, 32.3 us)
Async XLA Ops:
  0.0 24.6 %copy-start.3 = (bf16[640,160]{0,1:T(8,128)(2,1)S(1)}, bf16[640,160]{0,1:T(8,128)(2,1)}, u32[]{:S(2)}) copy-start(bf16[640,160]{0,1:T(8,128)(2,1)} %param.9) | copy-start | bytes 614404
  0.0 24.8 %copy-start.1 = (bf16[128,5120]{1,0:T(8,128)(2,1)S(1)}, bf16[128,5120]{1,0:T(8,128)(2,1)}, u32[]{:S(2)}) copy-start(bf16[128,5120]{1,0:T(8,128)(2,1)} %param.12) | copy-start | bytes 3932164
  0.0 26.2 %collective-permute-start = (bf16[160,640]{1,0:T(8,128)(2,1)}, bf16[160,640]{1,0:T(8,128)(2,1)}, u32[]{:S(2)}, u32[]{:S(2)}) collective-permute-start(bf16[160,640]{1,0:T(8,128)(2,1)} %bitcast.115), channel_id=1, source_target_pairs={{0,56},{8,0},{16,8},{24,16},{32,24},{40,32},{48,40},{56,48},{1,57}... | collective-permute-start | bytes 614408 | tf_op jit(solution)/shard_map/ppermute | solution.py:16
  5.9 24.0 %collective-permute-start.1 = (bf16[160,640]{1,0:T(8,128)(2,1)}, bf16[160,640]{1,0:T(8,128)(2,1)}, u32[]{:S(2)}, u32[]{:S(2)}) collective-permute-start(bf16[160,640]{1,0:T(8,128)(2,1)} %bitcast.116), channel_id=1, source_target_pairs={{0,48},{8,56},{16,0},{24,8},{32,16},{40,24},{48,32},{56,40},{1,49}... | collective-permute-start | bytes 614408 | tf_op jit(solution)/shard_map/ppermute | solution.py:16
  7.3 34.2 %collective-permute-start.2 = (bf16[160,640]{1,0:T(8,128)(2,1)}, bf16[160,640]{1,0:T(8,128)(2,1)}, u32[]{:S(2)}, u32[]{:S(2)}) collective-permute-start(bf16[160,640]{1,0:T(8,128)(2,1)} %bitcast.117), channel_id=1, source_target_pairs={{0,40},{8,48},{16,56},{24,0},{32,8},{40,16},{48,24},{56,32},{1,41}... | collective-permute-start | bytes 614408 | tf_op jit(solution)/shard_map/ppermute | solution.py:16
  7.8 37.5 %collective-permute-start.3 = (bf16[160,640]{1,0:T(8,128)(2,1)}, bf16[160,640]{1,0:T(8,128)(2,1)}, u32[]{:S(2)}, u32[]{:S(2)}) collective-permute-start(bf16[160,640]{1,0:T(8,128)(2,1)} %bitcast.118), channel_id=1, source_target_pairs={{0,32},{8,40},{16,48},{24,56},{32,0},{40,8},{48,16},{56,24},{1,33}... | collective-permute-start | bytes 614408 | tf_op jit(solution)/shard_map/ppermute | solution.py:16
  12.8 33.5 %collective-permute-start.4 = (bf16[160,640]{1,0:T(8,128)(2,1)}, bf16[160,640]{1,0:T(8,128)(2,1)S(1)}, u32[]{:S(2)}, u32[]{:S(2)}) collective-permute-start(bf16[160,640]{1,0:T(8,128)(2,1)} %bitcast.119), channel_id=1, source_target_pairs={{0,24},{8,32},{16,40},{24,48},{32,56},{40,0},{48,8},{56,16},{1,25}... | collective-permute-start | bytes 614408 | tf_op jit(solution)/shard_map/ppermute | solution.py:16
  15.3 49.8 %all-to-all-start = ((s32[32,32,1]{1,2,0:T(1,128)}), s32[32,32,1]{1,2,0:T(1,128)S(1)}, u32[]{:S(2)}, u32[]{:S(2)}) async-start(s32[32,32,1]{1,2,0:T(1,128)} %bitcast.29), calls=%async_computation | async-start | bytes 32768 | tf_op jit(solution)/shard_map/all_to_all | solution.py:41
  26.2 20.1 %copy-start.5 = (bf16[256,640]{1,0:T(8,128)(2,1)S(1)}, bf16[256,640]{1,0:T(8,128)(2,1)}, u32[]{:S(2)}) copy-start(bf16[256,640]{1,0:T(8,128)(2,1)} %param.7) | copy-start | bytes 983044
  26.2 22.5 %collective-permute-start.5 = (bf16[160,640]{1,0:T(8,128)(2,1)S(1)}, bf16[160,640]{1,0:T(8,128)(2,1)S(1)}, u32[]{:S(2)}, u32[]{:S(2)}) collective-permute-start(bf16[160,640]{1,0:T(8,128)(2,1)S(1)} %bitcast.120), channel_id=1, source_target_pairs={{0,16},{8,24},{16,32},{24,40},{32,48},{40,56},{48,0},{56,8},{1,17}... | collective-permute-start | bytes 614408 | tf_op jit(solution)/shard_map/ppermute | solution.py:16
  29.9 19.2 %collective-permute-start.6 = (bf16[160,640]{1,0:T(8,128)(2,1)S(1)}, bf16[160,640]{1,0:T(8,128)(2,1)S(1)}, u32[]{:S(2)}, u32[]{:S(2)}) collective-permute-start(bf16[160,640]{1,0:T(8,128)(2,1)S(1)} %bitcast.121), channel_id=1, source_target_pairs={{0,8},{8,16},{16,24},{24,32},{32,40},{40,48},{48,56},{56,0},{1,9},... | collective-permute-start | bytes 614408 | tf_op jit(solution)/shard_map/ppermute | solution.py:16
  41.5 16.2 %collective-permute-start.9 = (bf16[256,640]{1,0:T(8,128)(2,1)}, bf16[256,640]{1,0:T(8,128)(2,1)S(1)}, u32[]{:S(2)}, u32[]{:S(2)}) collective-permute-start(bf16[256,640]{1,0:T(8,128)(2,1)} %param.7), channel_id=1, source_target_pairs={{0,192},{64,0},{128,64},{192,128},{1,193},{65,1},{129,65},{193,129... | collective-permute-start | bytes 983048 | tf_op jit(solution)/shard_map/ppermute | solution.py:16
  45.2 16.8 %collective-permute-start.7 = (bf16[256,640]{1,0:T(8,128)(2,1)}, bf16[256,640]{1,0:T(8,128)(2,1)S(1)}, u32[]{:S(2)}, u32[]{:S(2)}) collective-permute-start(bf16[256,640]{1,0:T(8,128)(2,1)} %param.7), channel_id=1, source_target_pairs={{0,64},{64,128},{128,192},{192,0},{1,65},{65,129},{129,193},{193,1... | collective-permute-start | bytes 983048 | tf_op jit(solution)/shard_map/ppermute | solution.py:16
  46.3 17.2 %collective-permute-start.8 = (bf16[256,640]{1,0:T(8,128)(2,1)S(1)}, bf16[256,640]{1,0:T(8,128)(2,1)S(1)}, u32[]{:S(2)}, u32[]{:S(2)}) collective-permute-start(bf16[256,640]{1,0:T(8,128)(2,1)S(1)} %copy-done.5), channel_id=1, source_target_pairs={{0,128},{64,192},{128,0},{192,64},{1,129},{65,193},{129,1},{193,65... | collective-permute-start | bytes 983048 | tf_op jit(solution)/shard_map/ppermute | solution.py:16
  65.1 5.0 %copy-start.2 = (bf16[1280,256]{0,1:T(8,128)(2,1)S(1)}, bf16[1280,256]{0,1:T(8,128)(2,1)}, u32[]{:S(2)}) copy-start(bf16[1280,256]{0,1:T(8,128)(2,1)} %convolution_convert_fusion.3) | copy-start | bytes 1966084
  65.1 22.5 %all-to-all-start.1 = ((bf16[128,8,640]{0,2,1:T(8,128)(2,1)}), bf16[128,8,640]{0,2,1:T(8,128)(2,1)}, u32[]{:S(2)}, u32[]{:S(2)}) async-start(bf16[128,8,640]{0,2,1:T(8,128)(2,1)} %bitcast.30), calls=%async_computation.1 | async-start | bytes 2621440 | tf_op jit(solution)/shard_map/all_to_all | solution.py:51
  73.2 28.7 %collective-permute-start.10 = (bf16[4,4,32,1280]{3,2,1,0:T(8,128)(2,1)}, bf16[4,4,32,1280]{3,2,1,0:T(8,128)(2,1)}, u32[]{:S(2)}, u32[]{:S(2)}) collective-permute-start(bf16[4,4,32,1280]{3,2,1,0:T(8,128)(2,1)} %dynamic-slice_bitcast_fusion), channel_id=1, source_target_pairs={{0,1},{1,0},{2,3},{3,2},{4,5},{5,4},{6,7},{7,6},{8,9},{9,8},{10,11... | collective-permute-start | bytes 3932168 | tf_op jit(solution)/shard_map/ppermute | solution.py:16
  94.4 47.5 %all-to-all-start.2 = ((bf16[32,32,640]{2,1,0:T(8,128)(2,1)}), bf16[32,32,640]{2,1,0:T(8,128)(2,1)}, u32[]{:S(2)}, u32[]{:S(2)}) async-start(bf16[32,32,640]{2,1,0:T(8,128)(2,1)} %bitcast.104), calls=%async_computation.2 | async-start | bytes 2621440 | tf_op jit(solution)/shard_map/all_to_all | solution.py:55
  104.7 23.4 %copy-start.4 = (bf16[640]{0:T(1024)(128)(2,1)S(1)}, bf16[640]{0:T(1024)(128)(2,1)}, u32[]{:S(2)}) copy-start(bf16[640]{0:T(1024)(128)(2,1)} %param.10) | copy-start | bytes 3844
  104.7 10.7 %collective-permute-start.11 = (bf16[4,32,1280]{2,1,0:T(8,128)(2,1)S(1)}, bf16[4,32,1280]{2,1,0:T(8,128)(2,1)S(1)}, u32[]{:S(2)}, u32[]{:S(2)}) collective-permute-start(bf16[4,32,1280]{2,1,0:T(8,128)(2,1)S(1)} %get-tuple-element.5), channel_id=1, source_target_pairs={{0,2},{2,4},{4,6},{6,0},{1,3},{3,5},{5,7},{7,1},{8,10},{10,12},{12... | collective-permute-start | bytes 983048 | tf_op jit(solution)/shard_map/ppermute | solution.py:16
  104.8 12.3 %collective-permute-start.12 = (bf16[4,32,1280]{2,1,0:T(8,128)(2,1)S(1)}, bf16[4,32,1280]{2,1,0:T(8,128)(2,1)S(1)}, u32[]{:S(2)}, u32[]{:S(2)}) collective-permute-start(bf16[4,32,1280]{2,1,0:T(8,128)(2,1)S(1)} %get-tuple-element.7), channel_id=1, source_target_pairs={{0,4},{2,6},{4,0},{6,2},{1,5},{3,7},{5,1},{7,3},{8,12},{10,14},{12... | collective-permute-start | bytes 983048 | tf_op jit(solution)/shard_map/ppermute | solution.py:16
  108.3 14.1 %collective-permute-start.13 = (bf16[4,32,1280]{2,1,0:T(8,128)(2,1)S(1)}, bf16[4,32,1280]{2,1,0:T(8,128)(2,1)S(1)}, u32[]{:S(2)}, u32[]{:S(2)}) collective-permute-start(bf16[4,32,1280]{2,1,0:T(8,128)(2,1)S(1)} %get-tuple-element.6), channel_id=1, source_target_pairs={{0,6},{2,0},{4,2},{6,4},{1,7},{3,1},{5,3},{7,5},{8,14},{10,8},{12,... | collective-permute-start | bytes 983048 | tf_op jit(solution)/shard_map/ppermute | solution.py:16
  123.6 18.1 %collective-permute-start.14 = (bf16[32,1280]{1,0:T(8,128)(2,1)S(1)}, bf16[32,1280]{1,0:T(8,128)(2,1)S(1)}, u32[]{:S(2)}, u32[]{:S(2)}) collective-permute-start(bf16[32,1280]{1,0:T(8,128)(2,1)S(1)} %get-tuple-element.15), channel_id=1, source_target_pairs={{0,192},{64,0},{128,64},{192,128},{1,193},{65,1},{129,65},{193,129... | collective-permute-start | bytes 245768 | tf_op jit(solution)/shard_map/ppermute | solution.py:16
  126.4 15.3 %collective-permute-start.15 = (bf16[32,1280]{1,0:T(8,128)(2,1)S(1)}, bf16[32,1280]{1,0:T(8,128)(2,1)S(1)}, u32[]{:S(2)}, u32[]{:S(2)}) collective-permute-start(bf16[32,1280]{1,0:T(8,128)(2,1)S(1)} %get-tuple-element.14), channel_id=1, source_target_pairs={{0,128},{64,192},{128,0},{192,64},{1,129},{65,193},{129,1},{193,65... | collective-permute-start | bytes 245768 | tf_op jit(solution)/shard_map/ppermute | solution.py:16
  127.2 14.5 %collective-permute-start.16 = (bf16[32,1280]{1,0:T(8,128)(2,1)S(1)}, bf16[32,1280]{1,0:T(8,128)(2,1)S(1)}, u32[]{:S(2)}, u32[]{:S(2)}) collective-permute-start(bf16[32,1280]{1,0:T(8,128)(2,1)S(1)} %get-tuple-element.13), channel_id=1, source_target_pairs={{0,64},{64,128},{128,192},{192,0},{1,65},{65,129},{129,193},{193,1... | collective-permute-start | bytes 245768 | tf_op jit(solution)/shard_map/ppermute | solution.py:16
  144.5 11.1 %all-to-all-start.3 = ((bf16[8,32,640]{2,1,0:T(8,128)(2,1)}), bf16[8,32,640]{2,1,0:T(8,128)(2,1)S(1)}, u32[]{:S(2)}, u32[]{:S(2)}) async-start(bf16[8,32,640]{2,1,0:T(8,128)(2,1)} %bitcast.35), calls=%async_computation.3 | async-start | bytes 655360 | tf_op jit(solution)/shard_map/all_to_all | solution.py:57
  156.9 10.7 %collective-permute-start.17 = (bf16[32,5120]{1,0:T(8,128)(2,1)S(1)}, bf16[32,5120]{1,0:T(8,128)(2,1)S(1)}, u32[]{:S(2)}, u32[]{:S(2)}) collective-permute-start(bf16[32,5120]{1,0:T(8,128)(2,1)S(1)} %subtract_convert_fusion), channel_id=1, source_target_pairs={{0,2},{2,4},{4,6},{6,0},{1,3},{3,5},{5,7},{7,1},{8,10},{10,12},{12... | collective-permute-start | bytes 983048 | tf_op jit(solution)/shard_map/ppermute | solution.py:16
  156.9 12.3 %collective-permute-start.18 = (bf16[32,5120]{1,0:T(8,128)(2,1)S(1)}, bf16[32,5120]{1,0:T(8,128)(2,1)S(1)}, u32[]{:S(2)}, u32[]{:S(2)}) collective-permute-start(bf16[32,5120]{1,0:T(8,128)(2,1)S(1)} %subtract_convert_fusion), channel_id=1, source_target_pairs={{0,4},{2,6},{4,0},{6,2},{1,5},{3,7},{5,1},{7,3},{8,12},{10,14},{12... | collective-permute-start | bytes 983048 | tf_op jit(solution)/shard_map/ppermute | solution.py:16
  160.5 14.1 %collective-permute-start.19 = (bf16[32,5120]{1,0:T(8,128)(2,1)S(1)}, bf16[32,5120]{1,0:T(8,128)(2,1)S(1)}, u32[]{:S(2)}, u32[]{:S(2)}) collective-permute-start(bf16[32,5120]{1,0:T(8,128)(2,1)S(1)} %subtract_convert_fusion), channel_id=1, source_target_pairs={{0,6},{2,0},{4,2},{6,4},{1,7},{3,1},{5,3},{7,5},{8,14},{10,8},{12,... | collective-permute-start | bytes 983048 | tf_op jit(solution)/shard_map/ppermute | solution.py:16
  175.8 7.0 %collective-permute-start.20 = (bf16[4,32,5120]{2,1,0:T(8,128)(2,1)}, bf16[4,32,5120]{2,1,0:T(8,128)(2,1)}, u32[]{:S(2)}, u32[]{:S(2)}) collective-permute-start(bf16[4,32,5120]{2,1,0:T(8,128)(2,1)} %pad_maximum_fusion.1), channel_id=1, source_target_pairs={{0,1},{1,0},{2,3},{3,2},{4,5},{5,4},{6,7},{7,6},{8,9},{9,8},{10,11... | collective-permute-start | bytes 3932168 | tf_op jit(solution)/shard_map/ppermute | solution.py:16
  176.1 6.6 %slice-start = ((s8[6553600]{0:T(1024)(128)(4,1)}), s8[2359296]{0:T(1024)(128)(4,1)S(1)}, s32[]{:S(2)}) async-start(s8[6553600]{0:T(1024)(128)(4,1)} %bitcast.100), calls=%async_computation.5 | async-start | bytes 4718592
  178.1 4.6 %slice-start.1 = ((s8[6553600]{0:T(1024)(128)(4,1)}), s8[4194304]{0:T(1024)(128)(4,1)S(1)}, s32[]{:S(2)}) async-start(s8[6553600]{0:T(1024)(128)(4,1)} %bitcast.100), calls=%async_computation.6 | async-start | bytes 8388608
  (1 other events, 1.1 us)
